TPU v7x, 256 devices: a whole 4x4x8 slice. The times are simulated.
256 devices in a mesh: shard: 64 (over y, z, core), group: 4 (over x).
Axes of the slice: x: 4, y: 4, z: 8, core: 2. Of those that a mesh axis runs over, the one named last changes fastest.
Arguments:
- embeddings: bfloat16 [1024, 512, 768], P(('shard', 'group')), may hold values from -50 to 50, as said below
- partners: int32 [1024, 8], P(('shard', 'group')), may hold values from -1 to 1023, as said below
- cluster: int32 [1024], P(('shard', 'group')), may hold values from 0 to 255, never falling along the last dimension, each value on 1 to 8 neighbouring positions
- counts: int32 [1024], P(('shard', 'group')), may hold values from 128 to 512
Outputs:
- maxsim: float32 [1024, 512], P(('shard', 'group'))
Inputs may be any that keep to these rules, and one draw needn't show every extreme that they name: `partners`: entry k of block a's list is a + k or -1; entry 0 is always a itself; no entry passes the last block. Never falling along the blocks; each cluster spans 1 to 8 consecutive blocks. Real-valued embeddings of no particular norm.
All inputs are finite; a program needn't handle non-finite values.
Results may differ from a plain program's by a relative error of at most 0.0007.
Values may be sent and summed in bfloat16 or wider, within the bound.
A program may use at most 64 MiB of HBM per device.

v0:
```python
from functools import partial

import jax
import jax.numpy as jnp
from jax import lax
from jax.sharding import PartitionSpec as P


def from_behind(value, axis, steps):
    count = lax.axis_size(axis)
    initial, last = (max(0, -steps), min(count, count - steps))
    return lax.ppermute(value, axis, [(source, source + steps) for source in range(initial, last)])


def per_device(embeddings, partners, cluster, counts):
    blocks_here = embeddings.shape[0]
    block_rows = embeddings.shape[1]
    slots = partners.shape[1]
    devices = lax.axis_size(("shard", "group"))
    reach_dev = (blocks_here + slots - 2) // blocks_here
    own_index = lax.axis_index(("shard", "group"))
    floats = embeddings.astype(jnp.float32)
    unit_rows = (
        floats * lax.rsqrt(jnp.sum(floats * floats, axis=-1, keepdims=True) + 1e-06)
    ).astype(jnp.bfloat16)
    block_info = jnp.concatenate([partners + 1, cluster[:, None], counts[:, None]], axis=1)
    lowest = 0
    fetched_units = []
    fetched_info = []
    for offset in range(lowest, reach_dev + 1):
        if offset == 0:
            fetched_units.append(unit_rows)
            fetched_info.append(block_info)
        else:
            got_unit, got_info = from_behind((unit_rows, block_info), ("shard", "group"), -offset)
            fetched_units.append(got_unit)
            fetched_info.append(got_info)
    window_unit = jnp.concatenate(fetched_units, axis=0)
    window_info = jnp.concatenate(fetched_info, axis=0)
    window_blocks = window_unit.shape[0]
    window_cluster = window_info[:, slots]
    window_count = window_info[:, slots + 1]
    row_ids = jnp.arange(block_rows, dtype=jnp.int32)

    def score_pair(offset, slot_k, local_block, running):
        slot_a = (offset - lowest) * blocks_here + local_block
        partner_link = window_info[slot_a, slot_k]
        partner = partner_link - 1
        first_block = (own_index + offset) * blocks_here + local_block
        device_b = jnp.floor_divide(partner, blocks_here)
        slot_b = jnp.clip(
            (device_b - own_index - lowest) * blocks_here + jnp.remainder(partner, blocks_here),
            0,
            window_blocks - 1,
        )
        active = (partner_link > 0) & (window_cluster[slot_b] == window_cluster[slot_a])

        def update(current):
            left_unit = lax.dynamic_index_in_dim(window_unit, slot_a, 0, keepdims=False)
            right_unit = lax.dynamic_index_in_dim(window_unit, slot_b, 0, keepdims=False)
            scores = lax.dot_general(
                left_unit, right_unit, (((1,), (1,)), ((), ())), preferred_element_type=jnp.float32
            )
            allowed = (row_ids[:, None] < window_count[slot_a]) & (
                row_ids[None, :] < window_count[slot_b]
            )
            allowed = allowed & jnp.logical_not(
                (partner == first_block) & (row_ids[:, None] == row_ids[None, :])
            )
            scores = jnp.where(allowed, scores, jnp.float32(-2.0))
            current = current.at[slot_a].max(jnp.max(scores, axis=1))
            current = current.at[slot_b].max(jnp.max(scores, axis=0))
            return current

        def unchanged(current):
            return current

        return lax.cond(active, update, unchanged, running)

    best_sim = jnp.full((window_blocks, block_rows), -1.0, jnp.float32)
    offset = 0
    for slot_k in range(slots):
        best_sim = lax.fori_loop(0, blocks_here, partial(score_pair, offset, slot_k), best_sim)
    per_slot = best_sim.reshape(window_blocks // blocks_here, blocks_here, block_rows)
    own_best = per_slot[-lowest]
    combined = own_best
    for offset in range(lowest, reach_dev + 1):
        if offset != 0:
            arrived = from_behind(per_slot[offset - lowest], ("shard", "group"), offset)
            source = own_index - offset
            arrived = jnp.where((source >= 0) & (source < devices), arrived, jnp.float32(-1.0))
            combined = jnp.maximum(combined, arrived)
    return jnp.where(row_ids[None, :] < counts[:, None], combined, jnp.float32(0.0))


def solution(mesh):
    return jax.shard_map(
        per_device,
        mesh=mesh,
        in_specs=(
            P(("shard", "group"), None, None),
            P(("shard", "group"), None),
            P(("shard", "group")),
            P(("shard", "group")),
        ),
        out_specs=P(("shard", "group"), None),
        check_vma=False,
    )
```

profile of v0, /device:TPU:41, one launch (start us, length us, event | category | flops | bytes accessed | tf_op | source)
XLA Modules:
  0.0 509.5 jit_solution(4956636225431783974)
XLA Ops:
  0.0 2.6 fusion.56
  2.6 2.5 fusion.57
  5.1 4.9 collective-permute-start.2
  10.1 2.7 collective-permute-start.3
  13.1 3.0 collective-permute-start
  16.1 2.5 collective-permute-start.1
  18.6 126.8 %collective-permute-done = s32[4,10]{1,0:T(4,128)S(1)} collective-permute-done((s32[4,10]{1,0:T(4,128)S(1)}, s32[4,10]{1,0:T(4,128)S(1)}, u32[]{:S(2)}, u32[]{:S(2)}) %collective-permute-start) | collective-permute-done | bytes 192 | tf_op jit(solution)/shard_map/ppermute | solution.py:12
  145.8 7.8 %pad_maximum_fusion = bf16[12,512,768]{2,1,0:T(8,128)(2,1)} fusion(bf16[4,512,768]{2,1,0:T(8,128)(2,1)} %collective-permute-done.3, bf16[4,512,768]{2,1,0:T(8,128)(2,1)} %collective-permute-done.2, bf16[4,512,768]{2,1,0:T(8,128)(2,1)S(1)} %fusion.57), kind=kLoop, calls=%fused_computation.128 | loop fusion | flops 9437184 | bytes 18874368 | tf_op jit(solution)/shard_map/concatenate | solution.py:38
  153.5 52.3 %while.184 = (s32[]{:T(128)}, f32[12,512]{1,0:T(8,128)S(1)}, s32[12,10]{1,0:T(8,128)S(1)}, s32[]{:T(128)}, s32[12]{0:T(128)S(1)}, /*index=5*/s32[12]{0:T(128)S(1...) while((s32[]{:T(128)}, f32[12,512]{1,0:T(8,128)S(1)}, ...), condition=%wide.region_8.9_spmd.clone.clone, body=%wide.region_1.8_spmd.clone.clone.sunk | while | flops 404752448 | bytes 1611464 | solution.py:83
  159.2 7.4 %conditional.32 = (f32[12,512]{1,0:T(8,128)S(1)}) conditional(s32[]{:T(128)} %convert_element_type.127, f32[12,512]{1,0:T(8,128)S(1)} %get-tuple-element.3658, (s32[]{:T(128)}, f32[12,512]{1,0:T(8,128)S(1)}, s32[12]{0:T(128)S(1)}, s32[512]{0:T(512)S(1)}, s32[]{:T(128)}, /*index=5*/s32[512]{0:T(512)S(1)}, s32[]{:T(128)}, s32[]{:T(128)}, ...), branch_computations={%region_2.2_spmd, %region_3.7_spmd} | conditional | flops 404752416 | bytes 1608874 | solution.py:78
  172.3 7.4 %conditional.32 = (f32[12,512]{1,0:T(8,128)S(1)}) conditional(s32[]{:T(128)} %convert_element_type.127, f32[12,512]{1,0:T(8,128)S(1)} %get-tuple-element.3658, (s32[]{:T(128)}, f32[12,512]{1,0:T(8,128)S(1)}, s32[12]{0:T(128)S(1)}, s32[512]{0:T(512)S(1)}, s32[]{:T(128)}, /*index=5*/s32[512]{0:T(512)S(1)}, s32[]{:T(128)}, s32[]{:T(128)}, ...), branch_computations={%region_2.2_spmd, %region_3.7_spmd} | conditional | flops 404752416 | bytes 1608874 | solution.py:78
  174.7 2.2 fusion.58
  185.4 7.4 %conditional.32 = (f32[12,512]{1,0:T(8,128)S(1)}) conditional(s32[]{:T(128)} %convert_element_type.127, f32[12,512]{1,0:T(8,128)S(1)} %get-tuple-element.3658, (s32[]{:T(128)}, f32[12,512]{1,0:T(8,128)S(1)}, s32[12]{0:T(128)S(1)}, s32[512]{0:T(512)S(1)}, s32[]{:T(128)}, /*index=5*/s32[512]{0:T(512)S(1)}, s32[]{:T(128)}, s32[]{:T(128)}, ...), branch_computations={%region_2.2_spmd, %region_3.7_spmd} | conditional | flops 404752416 | bytes 1608874 | solution.py:78
  198.5 7.4 %conditional.32 = (f32[12,512]{1,0:T(8,128)S(1)}) conditional(s32[]{:T(128)} %convert_element_type.127, f32[12,512]{1,0:T(8,128)S(1)} %get-tuple-element.3658, (s32[]{:T(128)}, f32[12,512]{1,0:T(8,128)S(1)}, s32[12]{0:T(128)S(1)}, s32[512]{0:T(512)S(1)}, s32[]{:T(128)}, /*index=5*/s32[512]{0:T(512)S(1)}, s32[]{:T(128)}, s32[]{:T(128)}, ...), branch_computations={%region_2.2_spmd, %region_3.7_spmd} | conditional | flops 404752416 | bytes 1608874 | solution.py:78
  205.9 30.5 %while.185 = (s32[]{:T(128)}, f32[12,512]{1,0:T(8,128)S(1)}, s32[12,10]{1,0:T(8,128)S(1)}, s32[]{:T(128)}, s32[12]{0:T(128)S(1)}, /*index=5*/s32[12]{0:T(128)S(1...) while((s32[]{:T(128)}, f32[12,512]{1,0:T(8,128)S(1)}, ...), condition=%wide.region_16.17_spmd.clone.clone, body=%wide.region_9.16_spmd.clone.clone.sunk | while | flops 404752448 | bytes 1611464 | solution.py:83
  223.2 7.4 %conditional.33 = (f32[12,512]{1,0:T(8,128)S(1)}) conditional(s32[]{:T(128)} %convert_element_type.128, f32[12,512]{1,0:T(8,128)S(1)} %get-tuple-element.3706, (s32[]{:T(128)}, f32[12,512]{1,0:T(8,128)S(1)}, s32[12]{0:T(128)S(1)}, s32[512]{0:T(512)S(1)}, s32[]{:T(128)}, /*index=5*/s32[512]{0:T(512)S(1)}, s32[]{:T(128)}, s32[]{:T(128)}, ...), branch_computations={%region_10.10_spmd, %region_11.15_spmd} | conditional | flops 404752416 | bytes 1608874 | solution.py:78
  236.3 23.1 %while.186 = (s32[]{:T(128)}, f32[12,512]{1,0:T(8,128)S(1)}, s32[12,10]{1,0:T(8,128)S(1)}, s32[]{:T(128)}, s32[12]{0:T(128)S(1)}, /*index=5*/s32[12]{0:T(128)S(1...) while((s32[]{:T(128)}, f32[12,512]{1,0:T(8,128)S(1)}, ...), condition=%wide.region_24.25_spmd.clone.clone, body=%wide.region_17.24_spmd.clone.clone.sunk | while | flops 404752448 | bytes 1611464 | solution.py:83
  259.4 23.1 %while.187 = (s32[]{:T(128)}, f32[12,512]{1,0:T(8,128)S(1)}, s32[12,10]{1,0:T(8,128)S(1)}, s32[]{:T(128)}, s32[12]{0:T(128)S(1)}, /*index=5*/s32[12]{0:T(128)S(1...) while((s32[]{:T(128)}, f32[12,512]{1,0:T(8,128)S(1)}, ...), condition=%wide.region_32.33_spmd.clone.clone, body=%wide.region_25.32_spmd.clone.clone.sunk | while | flops 404752448 | bytes 1611464 | solution.py:83
  282.5 23.1 %while.188 = (s32[]{:T(128)}, f32[12,512]{1,0:T(8,128)S(1)}, s32[12,10]{1,0:T(8,128)S(1)}, s32[]{:T(128)}, s32[12]{0:T(128)S(1)}, /*index=5*/s32[12]{0:T(128)S(1...) while((s32[]{:T(128)}, f32[12,512]{1,0:T(8,128)S(1)}, ...), condition=%wide.region_40.41_spmd.clone.clone, body=%wide.region_33.40_spmd.clone.clone.sunk | while | flops 404752448 | bytes 1611464 | solution.py:83
  305.6 23.1 %while.189 = (s32[]{:T(128)}, f32[12,512]{1,0:T(8,128)S(1)}, s32[12,10]{1,0:T(8,128)S(1)}, s32[]{:T(128)}, s32[12]{0:T(128)S(1)}, /*index=5*/s32[12]{0:T(128)S(1...) while((s32[]{:T(128)}, f32[12,512]{1,0:T(8,128)S(1)}, ...), condition=%wide.region_48.49_spmd.clone.clone, body=%wide.region_41.48_spmd.clone.clone.sunk | while | flops 404752448 | bytes 1611464 | solution.py:83
  328.7 23.1 %while.190 = (s32[]{:T(128)}, f32[12,512]{1,0:T(8,128)S(1)}, s32[12,10]{1,0:T(8,128)S(1)}, s32[]{:T(128)}, s32[12]{0:T(128)S(1)}, /*index=5*/s32[12]{0:T(128)S(1...) while((s32[]{:T(128)}, f32[12,512]{1,0:T(8,128)S(1)}, ...), condition=%wide.region_56.57_spmd.clone.clone, body=%wide.region_49.56_spmd.clone.clone.sunk | while | flops 404752448 | bytes 1611464 | solution.py:83
  351.8 23.1 %while.191 = (s32[]{:T(128)}, f32[12,512]{1,0:T(8,128)S(1)}, s32[12,10]{1,0:T(8,128)S(1)}, s32[]{:T(128)}, s32[12]{0:T(128)S(1)}, /*index=5*/s32[12]{0:T(128)S(1...) while((s32[]{:T(128)}, f32[12,512]{1,0:T(8,128)S(1)}, ...), condition=%wide.region_64.65_spmd.clone.clone, body=%wide.region_57.64_spmd.clone.clone.sunk | while | flops 404752448 | bytes 1611464 | solution.py:83
  375.0 127.4 %collective-permute-start.4 = (f32[4,512]{1,0:T(4,128)S(1)}, f32[4,512]{1,0:T(4,128)S(1)}, u32[]{:S(2)}, u32[]{:S(2)}) collective-permute-start(f32[4,512]{1,0:T(4,128)S(1)} %get-tuple-element.3183), channel_id=1, source_target_pairs={{0,1},{1,2},{2,3},{3,4},{4,5},{5,6},{6,7},{7,8},{8,9},{9,10},{10,1... | collective-permute-start | bytes 24584 | tf_op jit(solution)/shard_map/ppermute | solution.py:12
  504.3 4.5 collective-permute-done.5
  (183 shorter events, 76.2 us)
Async XLA Ops:
  0.0 12.8 %copy-start.2 = (s32[4]{0:T(128)S(1)}, s32[4]{0:T(128)}, u32[]{:S(2)}) copy-start(s32[4]{0:T(128)} %param.70) | copy-start | bytes 52
  0.0 12.9 %copy-start = (s32[4]{0:T(128)S(1)}, s32[4]{0:T(128)}, u32[]{:S(2)}) copy-start(s32[4]{0:T(128)} %param.71) | copy-start | bytes 52
  0.0 13.0 %copy-start.1 = (s32[4,8]{1,0:T(4,128)S(1)}, s32[4,8]{1,0:T(4,128)}, u32[]{:S(2)}) copy-start(s32[4,8]{1,0:T(4,128)} %param.69) | copy-start | bytes 388
  5.1 140.6 %collective-permute-start.2 = (bf16[4,512,768]{2,1,0:T(8,128)(2,1)S(1)}, bf16[4,512,768]{2,1,0:T(8,128)(2,1)}, u32[]{:S(2)}, u32[]{:S(2)}) collective-permute-start(bf16[4,512,768]{2,1,0:T(8,128)(2,1)S(1)} %fusion.57), channel_id=1, source_target_pairs={{1,0},{2,1},{3,2},{4,3},{5,4},{6,5},{7,6},{8,7},{9,8},{10,9},{11,1... | collective-permute-start | bytes 9437192 | tf_op jit(solution)/shard_map/ppermute | solution.py:12
  10.1 135.7 %collective-permute-start.3 = (bf16[4,512,768]{2,1,0:T(8,128)(2,1)S(1)}, bf16[4,512,768]{2,1,0:T(8,128)(2,1)}, u32[]{:S(2)}, u32[]{:S(2)}) collective-permute-start(bf16[4,512,768]{2,1,0:T(8,128)(2,1)S(1)} %fusion.57), channel_id=1, source_target_pairs={{2,0},{3,1},{4,2},{5,3},{6,4},{7,5},{8,6},{9,7},{10,8},{11,9},{12,... | collective-permute-start | bytes 9437192 | tf_op jit(solution)/shard_map/ppermute | solution.py:12
  13.1 132.4 %collective-permute-start = (s32[4,10]{1,0:T(4,128)S(1)}, s32[4,10]{1,0:T(4,128)S(1)}, u32[]{:S(2)}, u32[]{:S(2)}) collective-permute-start(s32[4,10]{1,0:T(4,128)S(1)} %pad_add_fusion.17), channel_id=1, source_target_pairs={{1,0},{2,1},{3,2},{4,3},{5,4},{6,5},{7,6},{8,7},{9,8},{10,9},{11,1... | collective-permute-start | bytes 488 | tf_op jit(solution)/shard_map/ppermute | solution.py:12
  16.1 129.4 %collective-permute-start.1 = (s32[4,10]{1,0:T(4,128)S(1)}, s32[4,10]{1,0:T(4,128)S(1)}, u32[]{:S(2)}, u32[]{:S(2)}) collective-permute-start(s32[4,10]{1,0:T(4,128)S(1)} %pad_add_fusion.17), channel_id=1, source_target_pairs={{2,0},{3,1},{4,2},{5,3},{6,4},{7,5},{8,6},{9,7},{10,8},{11,9},{12,... | collective-permute-start | bytes 488 | tf_op jit(solution)/shard_map/ppermute | solution.py:12
  375.0 129.4 %collective-permute-start.4 = (f32[4,512]{1,0:T(4,128)S(1)}, f32[4,512]{1,0:T(4,128)S(1)}, u32[]{:S(2)}, u32[]{:S(2)}) collective-permute-start(f32[4,512]{1,0:T(4,128)S(1)} %get-tuple-element.3183), channel_id=1, source_target_pairs={{0,1},{1,2},{2,3},{3,4},{4,5},{5,6},{6,7},{7,8},{8,9},{9,10},{10,1... | collective-permute-start | bytes 24584 | tf_op jit(solution)/shard_map/ppermute | solution.py:12
  502.4 6.5 %collective-permute-start.5 = (f32[4,512]{1,0:T(4,128)S(1)}, f32[4,512]{1,0:T(4,128)S(1)}, u32[]{:S(2)}, u32[]{:S(2)}) collective-permute-start(f32[4,512]{1,0:T(4,128)S(1)} %get-tuple-element.3184), channel_id=1, source_target_pairs={{0,2},{1,3},{2,4},{3,5},{4,6},{5,7},{6,8},{7,9},{8,10},{9,11},{10,... | collective-permute-start | bytes 24584 | tf_op jit(solution)/shard_map/ppermute | solution.py:12
where the time goes:
time: 514 us; the launch traced here: 510 us
  loops' own time  146 us (28%)
  starting transfers between devices  143 us (28%)
  waiting for transfers between devices  131 us (25%)
  other arithmetic  53.3 us (10%)
  local copies, waits for them, and re-layouts  24.8 us (5%)
  matrix products  10.9 us (2%)
    another operation x8, loops' own time, per_device(): lax.fori_loop(0, blocks_here, partial(score_pair, offset, slot_k), best_sim)  143 us
    ppermute x6, starting transfers between devices, from_behind(): lax.ppermute(value, axis, [(source, source + steps) for source in range(i...  143 us
    ppermute x6, waiting for transfers between devices, from_behind(): lax.ppermute(value, axis, [(source, source + steps) for source in range(i...  131 us
    sub x32, other arithmetic, score_pair(): partner = partner_link - 1  20.7 us
    dynamic_slice x32, local copies, waits for them, and re-layouts, score_pair(): window_cluster[slot_a]  20.6 us
    another operation x15, other arithmetic  12.9 us
    dot_general x5, matrix products, update(): lax.dot_general(left_unit, right_unit, (((1,), (1,)), ((), ())), preferre...  10.9 us
  transfers between devices with their start and end apart: 6, of which 2 were waited for; matrix products, arithmetic and copies ran while one was open for 0% of the time, Pallas kernels for 0%

commit v1 on v0

v1 whole, which is shorter than its diff:
```python
import functools

import jax
import jax.numpy as jnp
from jax import lax
from jax.experimental import pallas as pl
from jax.experimental.pallas import tpu as pltpu
from jax.sharding import PartitionSpec as P

MESH = pl.DeviceIdType.MESH
AXES = ("shard", "group")
CHUNK = 256
PER = 4
SIDE = 8
LOW = -4.0


def scored(slot, rows, partner, window):
    return lax.dot_general(
        window[slot, rows, :],
        window[partner],
        (((1,), (1,)), ((), ())),
        preferred_element_type=jnp.float32,
    )


def fold_rows(scores):
    rows, columns = scores.shape
    return jnp.max(scores.reshape(rows // 8, 8, columns), axis=0)


def fold_columns(scores):
    best = scores[:, 0:128]
    for start in range(128, scores.shape[1], 128):
        best = jnp.maximum(best, scores[:, start : start + 128])
    return best


def kernel(
    devices,
    emb,
    partners,
    cluster,
    counts,
    out,
    window,
    info,
    facts,
    col_best,
    row_part,
    row_best,
    sent_best,
    got_best,
    load_sem,
    emb_send,
    emb_recv,
    info_send,
    info_recv,
    facts_sem,
    best_send,
    best_recv,
):
    rows_all = window.shape[1]
    chunks = rows_all // CHUNK
    shards = lax.axis_size("shard")
    groups = lax.axis_size("group")
    me = lax.axis_index("shard") * groups + lax.axis_index("group")
    total = shards * groups

    def place(index):
        index = lax.rem(index + total, total)
        return (lax.div(index, groups), lax.rem(index, groups))

    right, left = place(me + 1), place(me - 1)

    def leftwards(index):
        return lax.rem(lax.div(index + total, groups), 2) == 0

    right_meets_here = leftwards(me)
    left_meets_here = jnp.logical_not(leftwards(me + total - 1))

    barrier = pltpu.get_barrier_semaphore()
    for neighbour in (left, right):
        pl.semaphore_signal(barrier, inc=1, device_id=neighbour, device_id_type=MESH)

    def load_own(block):
        return pltpu.make_async_copy(emb.at[block], window.at[PER + block], load_sem.at[block])

    for block in range(PER):
        load_own(block).start()

    info[1] = jnp.zeros(info.shape[1:], jnp.int32)
    info[1, 0:PER, 0:SIDE] = partners[...]
    for block in range(PER):
        info[1, PER + block : PER + block + 1, :] = jnp.full((1, 128), cluster[block], jnp.int32)
        info[1, 2 * PER + block : 2 * PER + block + 1, :] = jnp.full((1, 128), counts[block], jnp.int32)
    pl.semaphore_wait(barrier, 2)

    info_left = pltpu.make_async_remote_copy(
        src_ref=info.at[1], dst_ref=info.at[2], send_sem=info_send.at[0], recv_sem=info_recv.at[0],
        device_id=left, device_id_type=MESH,
    )
    info_right = pltpu.make_async_remote_copy(
        src_ref=info.at[1], dst_ref=info.at[0], send_sem=info_send.at[1], recv_sem=info_recv.at[1],
        device_id=right, device_id_type=MESH,
    )
    info_left.start()
    info_right.start()

    def push(step, chunk, leftward):
        block = step if leftward else PER - 1 - step
        slot = 2 * PER + step if leftward else PER - 1 - step
        rows = pl.ds(chunk * CHUNK, CHUNK)
        side = 0 if leftward else 1
        return pltpu.make_async_remote_copy(
            src_ref=emb.at[block, rows, :],
            dst_ref=window.at[slot, rows, :],
            send_sem=emb_send.at[side, step, chunk],
            recv_sem=emb_recv.at[side, step, chunk],
            device_id=left if leftward else right,
            device_id_type=MESH,
        )

    sends_last_left = jnp.logical_not(left_meets_here)
    sends_last_right = jnp.logical_not(right_meets_here)
    for step in range(PER - 1):
        for chunk in range(chunks):
            push(step, chunk, True).start()
            push(step, chunk, False).start()

    @pl.when(sends_last_left)
    def _():
        for chunk in range(chunks):
            push(PER - 1, chunk, True).start()

    @pl.when(sends_last_right)
    def _():
        for chunk in range(chunks):
            push(PER - 1, chunk, False).start()

    col_best[...] = jnp.full(col_best.shape, LOW, jnp.float32)
    row_best[...] = jnp.full(row_best.shape, LOW, jnp.float32)
    for block in range(PER):
        load_own(block).wait()
    info_left.wait()
    info_right.wait()
    to_facts = pltpu.make_async_copy(info, facts, facts_sem)
    to_facts.start()
    to_facts.wait()

    def count_of(slot):
        return facts[lax.div(slot, PER), 2 * PER + lax.rem(slot, PER), 0]

    def penalty(slot, other):
        first, second = jnp.minimum(slot, other), jnp.maximum(slot, other)
        device_a, block_a = lax.div(first, PER), lax.rem(first, PER)
        device_b, block_b = lax.div(second, PER), lax.rem(second, PER)
        listed = facts[device_a, block_a, second - first] >= 0
        same = facts[device_a, PER + block_a, 0] == facts[device_b, PER + block_b, 0]
        return jnp.where(listed & same, jnp.float32(0.0), jnp.float32(LOW))

    def normalise(slot, chunk):
        rows = pl.ds(pl.multiple_of(chunk * CHUNK, CHUNK), CHUNK)
        floats = window[slot, rows, :].astype(jnp.float32)
        unit = floats * lax.rsqrt(jnp.sum(floats * floats, axis=-1, keepdims=True) + 1e-06)
        head = window[slot, 0:16, :].astype(jnp.float32)[0:1, :]
        head = jnp.where(chunk == 0, unit[0:1, :], head)
        ids = chunk * CHUNK + lax.broadcasted_iota(jnp.int32, (CHUNK, 1), 0)
        window[slot, rows, :] = jnp.where(ids < count_of(slot), unit, head).astype(jnp.bfloat16)

    def meet(slot, chunk, low, high):
        rows = pl.ds(pl.multiple_of(chunk * CHUNK, CHUNK), CHUNK)
        row_part[...] = jnp.full(row_part.shape, LOW, jnp.float32)

        def one(other, carry):
            scores = scored(slot, rows, other, window)
            cost = penalty(slot, other)
            col_best[other] = jnp.maximum(col_best[other], fold_rows(scores) + cost)
            row_part[...] = jnp.maximum(row_part[...], fold_columns(scores) + cost)
            return carry

        lax.fori_loop(low, high, one, 0)
        best = jnp.max(row_part[...].T, axis=0, keepdims=True)
        row_best[slot, :, rows] = jnp.broadcast_to(best, (8, CHUNK))

    def own_normalise(index, carry):
        normalise(PER + lax.div(index, chunks), lax.rem(index, chunks))
        return carry

    lax.fori_loop(0, PER * chunks, own_normalise, 0)

    def own_step(index, carry):
        slot, chunk = PER + lax.div(index, chunks), lax.rem(index, chunks)
        meet(slot, chunk, PER, slot)
        rows = pl.ds(pl.multiple_of(chunk * CHUNK, CHUNK), CHUNK)
        scores = scored(slot, rows, slot, window)
        row_ids = chunk * CHUNK + lax.broadcasted_iota(jnp.int32, scores.shape, 0)
        col_ids = lax.broadcasted_iota(jnp.int32, scores.shape, 1)
        allowed = (row_ids < count_of(slot)) & (row_ids != col_ids)
        scores = jnp.where(allowed, scores, jnp.float32(LOW))
        col_best[slot] = jnp.maximum(col_best[slot], fold_rows(scores) + penalty(slot, slot))
        return carry

    lax.fori_loop(0, PER * chunks, own_step, 0)

    def arrived(step, chunk, side, slot):
        rows = pl.ds(pl.multiple_of(chunk * CHUNK, CHUNK), CHUNK)
        return pltpu.make_async_remote_copy(
            src_ref=emb.at[0, rows, :],
            dst_ref=window.at[slot, rows, :],
            send_sem=emb_send.at[side, step, chunk],
            recv_sem=emb_recv.at[side, step, chunk],
            device_id=left,
            device_id_type=MESH,
        )

    def exchange_step(index, carry):
        step, side = lax.div(index, 2), lax.rem(index, 2)
        from_right = side == 0
        slot = jnp.where(from_right, 2 * PER + step, PER - 1 - step)
        with_own = jnp.where(from_right, right_meets_here, left_meets_here)
        crossing = jnp.where((step == 1) | (step == 2), 1, 0)
        left_crossing = jnp.where(step == 3, 0, jnp.where(step == 1, 2, 1))
        low = jnp.where(from_right, PER - crossing, jnp.where(with_own, PER, 2 * PER))
        high = jnp.where(from_right, jnp.where(with_own, 2 * PER, PER), 2 * PER + left_crossing)

        @pl.when((step < PER - 1) | with_own)
        def _():
            def one(chunk, inner):
                arrived(step, chunk, side, slot).wait_recv()
                normalise(slot, chunk)
                meet(slot, chunk, low, high)
                return inner

            lax.fori_loop(0, chunks, one, 0)

        return carry

    lax.fori_loop(0, 2 * PER, exchange_step, 0)

    def best_of(slot):
        return jnp.maximum(row_best[slot, 0:1, :], jnp.max(col_best[slot], axis=0, keepdims=True))

    for block in range(PER):
        sent_best[0, block : block + 1, :] = best_of(block)
        sent_best[1, block : block + 1, :] = best_of(2 * PER + block)
    best_left = pltpu.make_async_remote_copy(
        src_ref=sent_best.at[0], dst_ref=got_best.at[0], send_sem=best_send.at[0], recv_sem=best_recv.at[0],
        device_id=left, device_id_type=MESH,
    )
    best_right = pltpu.make_async_remote_copy(
        src_ref=sent_best.at[1], dst_ref=got_best.at[1], send_sem=best_send.at[1], recv_sem=best_recv.at[1],
        device_id=right, device_id_type=MESH,
    )
    best_left.start()
    best_right.start()

    for step in range(PER - 1):
        for chunk in range(chunks):
            push(step, chunk, True).wait_send()
            push(step, chunk, False).wait_send()

    @pl.when(sends_last_left)
    def _():
        for chunk in range(chunks):
            push(PER - 1, chunk, True).wait_send()

    @pl.when(sends_last_right)
    def _():
        for chunk in range(chunks):
            push(PER - 1, chunk, False).wait_send()

    best_left.wait()
    best_right.wait()
    ids = lax.broadcasted_iota(jnp.int32, (1, rows_all), 1)
    for block in range(PER):
        best = jnp.maximum(best_of(PER + block), jnp.float32(-1.0))
        best = jnp.maximum(best, got_best[0, block : block + 1, :])
        best = jnp.maximum(best, got_best[1, block : block + 1, :])
        out[block : block + 1, :] = jnp.where(ids < counts[block], best, jnp.float32(0.0))


def solution(mesh):
    devices = mesh.size

    def per_device(embeddings, partners, cluster, counts):
        blocks, rows, width = embeddings.shape
        chunks = rows // CHUNK
        return pl.pallas_call(
            functools.partial(kernel, devices),
            out_shape=jax.ShapeDtypeStruct((blocks, rows), jnp.float32),
            in_specs=[
                pl.BlockSpec(memory_space=pl.ANY),
                pl.BlockSpec(memory_space=pltpu.VMEM),
                pl.BlockSpec(memory_space=pltpu.SMEM),
                pl.BlockSpec(memory_space=pltpu.SMEM),
            ],
            out_specs=pl.BlockSpec(memory_space=pltpu.VMEM),
            scratch_shapes=[
                pltpu.VMEM((3 * PER, rows, width), jnp.bfloat16),
                pltpu.VMEM((3, 16, 128), jnp.int32),
                pltpu.SMEM((3, 16, 128), jnp.int32),
                pltpu.VMEM((3 * PER, 8, rows), jnp.float32),
                pltpu.VMEM((CHUNK, 128), jnp.float32),
                pltpu.VMEM((3 * PER, 8, rows), jnp.float32),
                pltpu.VMEM((2, PER, rows), jnp.float32),
                pltpu.VMEM((2, PER, rows), jnp.float32),
                pltpu.SemaphoreType.DMA((PER,)),
                pltpu.SemaphoreType.DMA((2, PER, chunks)),
                pltpu.SemaphoreType.DMA((2, PER, chunks)),
                pltpu.SemaphoreType.DMA((2,)),
                pltpu.SemaphoreType.DMA((2,)),
                pltpu.SemaphoreType.DMA,
                pltpu.SemaphoreType.DMA((2,)),
                pltpu.SemaphoreType.DMA((2,)),
            ],
            compiler_params=pltpu.CompilerParams(
                collective_id=0, has_side_effects=True, vmem_limit_bytes=40 * 2**20
            ),
        )(embeddings, partners, cluster, counts)

    return jax.shard_map(
        per_device,
        mesh=mesh,
        in_specs=(P(AXES, None, None), P(AXES, None), P(AXES), P(AXES)),
        out_specs=P(AXES, None),
        check_vma=False,
    )
```

time: 514 us -> 79.2 us (0.15)
  the two profiles are of different devices: /device:TPU:41 before, /device:TPU:0 now
where the time goes in v1:
time: 79.2 us; the launch traced here: 78.9 us
  Pallas kernels  74.4 us (94%)
  local copies, waits for them, and re-layouts  4.48 us (6%)
    pallas_call x1, Pallas kernels, per_device(): pl.pallas_call(functools.partial(kernel, devices), out_shape=jax.ShapeDty...  74.4 us
    unnamed x9, local copies, waits for them, and re-layouts  4.48 us

profile of v1, /device:TPU:0, one launch (start us, length us, event | category | flops | bytes accessed | tf_op | source)
XLA Modules:
  0.0 78.9 jit_solution(14499641877074603985)
XLA Ops:
  0.0 0.0 copy-start
  0.0 1.9 %copy-done = bf16[4,512,768]{2,1,0:T(8,128)(2,1)S(1)} copy-done((bf16[4,512,768]{2,1,0:T(8,128)(2,1)S(1)}, bf16[4,512,768]{2,1,0:T(8,128)(2,1)}, u32[]{:S(2)}) %copy-start) | copy-done | bytes 3145752
  1.9 0.0 copy-start.1
  1.9 0.7 copy-done.1
  2.6 0.0 copy-start.2
  2.6 0.7 copy-done.2
  3.2 0.0 copy-start.3
  3.2 0.7 copy-done.3
  3.9 74.4 %shard_map.46 = f32[4,512]{1,0:T(4,128)S(1)} custom-call(bf16[4,512,768]{2,1,0:T(8,128)(2,1)S(1)} %copy-done, s32[4,8]{1,0:T(4,128)S(1)} %copy-done.1, s32[4]{0:T(128)S(1)} %copy-done.2, s32[4]{0:T(128)S(1)} %copy-done.3), custom_call_target="tpu_custom_call" | custom-call | tf_op jit(solution)/shard_map/pallas_call | solution.py:289
  78.3 0.6 copy.6
Async XLA Ops:
  0.0 1.9 %copy-start = (bf16[4,512,768]{2,1,0:T(8,128)(2,1)S(1)}, bf16[4,512,768]{2,1,0:T(8,128)(2,1)}, u32[]{:S(2)}) copy-start(bf16[4,512,768]{2,1,0:T(8,128)(2,1)} %emb.1) | copy-start | bytes 9437188
  1.9 0.7 copy-start.1
  2.6 0.7 copy-start.2
  3.2 0.7 copy-start.3

commit v2 on v1

v2 whole, which is shorter than its diff:
```python
import jax
import jax.numpy as jnp
from jax import lax
from jax.experimental import pallas as pl
from jax.experimental.pallas import tpu as pltpu
from jax.sharding import PartitionSpec as P

MESH = pl.DeviceIdType.MESH
AXES = ("shard", "group")
PER = 4
SLOTS = 3 * PER
HALF = 256
LOW = -4.0
LEFT, OWN, RIGHT, MATE_R, MATE_L, BEHIND, AHEAD = range(7)
NEAR, NEXT, THIRD, FOURTH = range(4)
PIECES = ((0, HALF), (HALF, HALF))


def fold_rows(scores):
    rows, columns = scores.shape
    return jnp.max(scores.reshape(rows // 8, 8, columns), axis=0)


def fold_columns(scores):
    best = scores[:, 0:128]
    for start in range(128, scores.shape[1], 128):
        best = jnp.maximum(best, scores[:, start : start + 128])
    return best


def kernel(
    emb,
    partners_hbm,
    cluster_hbm,
    counts_hbm,
    out,
    window,
    raw,
    stage,
    swapped,
    partners,
    cluster,
    counts,
    info,
    facts,
    col_best,
    row_part,
    row_best,
    sent_best,
    got_best,
    load_sem,
    small_sem,
    stage_sem,
    emb_send,
    emb_recv,
    swap_send,
    swap_recv,
    pass_send,
    pass_recv,
    info_send,
    info_recv,
    facts_sem,
    best_send,
    best_recv,
):
    rows_all = window.shape[1]
    shards = lax.axis_size("shard")
    groups = lax.axis_size("group")
    total = shards * groups
    pool = 2 * groups
    me = lax.axis_index("shard") * groups + lax.axis_index("group")

    def place(index):
        index = lax.rem(index + total, total)
        return (lax.div(index, groups), lax.rem(index, groups))

    first_r = lax.rem(me, pool) < groups
    first_l = lax.rem(me + total - 1, pool) < groups
    mate_r = jnp.where(first_r, me + groups, me - groups)
    mate_l = jnp.where(first_l, me + groups, me - groups)
    where_is = {
        LEFT: place(me - 1),
        RIGHT: place(me + 1),
        MATE_R: place(mate_r),
        MATE_L: place(mate_l),
        BEHIND: place(mate_l - 1),
        AHEAD: place(mate_r + 1),
    }
    seen_as = {LEFT: RIGHT, RIGHT: LEFT, MATE_R: MATE_R, MATE_L: MATE_L, BEHIND: AHEAD, AHEAD: BEHIND}

    barrier = pltpu.get_barrier_semaphore()
    for role in where_is:
        pl.semaphore_signal(barrier, inc=1, device_id=where_is[role], device_id_type=MESH)

    small = [
        pltpu.make_async_copy(partners_hbm, partners, small_sem.at[0]),
        pltpu.make_async_copy(cluster_hbm, cluster, small_sem.at[1]),
        pltpu.make_async_copy(counts_hbm, counts, small_sem.at[2]),
    ]
    loads = [pltpu.make_async_copy(emb.at[block], window.at[PER + block], load_sem.at[block]) for block in range(PER)]
    stages = [
        pltpu.make_async_copy(emb.at[2], stage.at[0], stage_sem.at[0]),
        pltpu.make_async_copy(emb.at[1], stage.at[1], stage_sem.at[1]),
    ]
    for copy in small + loads + stages:
        copy.start()
    info[OWN] = jnp.zeros(info.shape[1:], jnp.int32)
    for copy in small:
        copy.wait()
    info[OWN, 0:PER, 0 : partners.shape[1]] = partners[...]
    for block in range(PER):
        info[OWN, PER + block : PER + block + 1, :] = jnp.full((1, 128), cluster[block], jnp.int32)
        info[OWN, 2 * PER + block : 2 * PER + block + 1, :] = jnp.full((1, 128), counts[block], jnp.int32)
    pl.semaphore_wait(barrier, len(where_is))

    def remote(source, target, send_sem, recv_sem, role):
        return pltpu.make_async_remote_copy(
            src_ref=source,
            dst_ref=target,
            send_sem=send_sem,
            recv_sem=recv_sem,
            device_id=where_is[role],
            device_id_type=MESH,
        )

    def push(step, side, piece):
        start, size = PIECES[piece]
        rows = pl.ds(start, size)
        block = step if side == 0 else PER - 1 - step
        source = stage.at[side, rows, :] if step == THIRD else emb.at[block, rows, :]
        return remote(
            source,
            raw.at[side, step, rows, :],
            emb_send.at[side, step, piece],
            emb_recv.at[side, step, piece],
            LEFT if side == 0 else RIGHT,
        )

    def pass_on(side, piece):
        rows = pl.ds(*PIECES[piece])
        return remote(
            raw.at[side, THIRD, rows, :],
            raw.at[side, FOURTH, rows, :],
            pass_send.at[side, piece],
            pass_recv.at[side, piece],
            MATE_R if side == 0 else MATE_L,
        )

    infos = [
        remote(info.at[OWN], info.at[seen_as[role]], info_send.at[role], info_recv.at[seen_as[role]], role)
        for role in where_is
    ]

    def swap(side, piece):
        rows = pl.ds(*PIECES[piece])
        return remote(
            emb.at[PER - 1 if side == 0 else 0, rows, :],
            swapped.at[side, rows, :],
            swap_send.at[side, piece],
            swap_recv.at[side, piece],
            MATE_L if side == 0 else MATE_R,
        )

    for copy in infos:
        copy.start()
    for piece in range(len(PIECES)):
        for side in range(2):
            swap(side, piece).start()

    for piece in range(len(PIECES)):
        for side in range(2):
            push(NEAR, side, piece).start()

    col_best[...] = jnp.full(col_best.shape, LOW, jnp.float32)
    row_best[...] = jnp.full(row_best.shape, LOW, jnp.float32)
    for copy in infos:
        copy.wait()
    to_facts = pltpu.make_async_copy(info, facts, facts_sem)
    to_facts.start()
    for copy in loads + stages:
        copy.wait()
    to_facts.wait()

    def cluster_of(device, block):
        return facts[device, PER + block, 0]

    def spans(device_a, device_b):
        head = cluster_of(device_a, 0)
        return head == cluster_of(device_b, 3), head == cluster_of(device_b, 2)

    def third_is_lent(is_first, spans_all, spans_three, mate_spans_all):
        keeps_left = spans_three & (is_first | jnp.logical_not(spans_all))
        return mate_spans_all & jnp.logical_not(keeps_left), mate_spans_all & keeps_left

    whole_r, three_r = spans(OWN, RIGHT)
    whole_mr, three_mr = spans(MATE_R, AHEAD)
    whole_l, three_l = spans(LEFT, OWN)
    whole_ml, three_ml = spans(BEHIND, MATE_L)
    r_left, r_right = third_is_lent(first_r, whole_r, three_r, whole_mr)
    mr_left, _ = third_is_lent(jnp.logical_not(first_r), whole_mr, three_mr, whole_r)
    l_left, l_right = third_is_lent(first_l, whole_l, three_l, whole_ml)
    _, ml_right = third_is_lent(jnp.logical_not(first_l), whole_ml, three_ml, whole_l)

    def slot_cost(slot):
        holds = jnp.where(slot == 2 * PER + THIRD, jnp.logical_not(r_left), True)
        holds = jnp.where(slot == 2 * PER + FOURTH, mr_left, holds)
        holds = jnp.where(slot == PER - 1 - THIRD, jnp.logical_not(l_right), holds)
        return jnp.where(slot == PER - 1 - FOURTH, ml_right, holds)

    def count_of(slot):
        return facts[lax.div(slot, PER), 2 * PER + lax.rem(slot, PER), 0]

    def penalty(slot, other):
        first, second = jnp.minimum(slot, other), jnp.maximum(slot, other)
        device_a, block_a = lax.div(first, PER), lax.rem(first, PER)
        device_b, block_b = lax.div(second, PER), lax.rem(second, PER)
        listed = facts[device_a, block_a, second - first] >= 0
        same = cluster_of(device_a, block_a) == cluster_of(device_b, block_b)
        held = slot_cost(slot) & slot_cost(other)
        return jnp.where(listed & same & held, jnp.float32(0.0), jnp.float32(LOW))

    def normalise(slot, start, size, load):
        rows = pl.ds(start, size)
        floats = load(rows).astype(jnp.float32)
        unit = floats * lax.rsqrt(jnp.sum(floats * floats, axis=-1, keepdims=True) + 1e-06)
        head = window[slot, 0:16, :].astype(jnp.float32)[0:1, :]
        head = jnp.where(start == 0, unit[0:1, :], head)
        ids = start + lax.broadcasted_iota(jnp.int32, (size, 1), 0)
        window[slot, rows, :] = jnp.where(ids < count_of(slot), unit, head).astype(jnp.bfloat16)

    def scored(slot, rows, other, columns):
        return lax.dot_general(
            window[slot, rows, :],
            window[other, columns, :],
            (((1,), (1,)), ((), ())),
            preferred_element_type=jnp.float32,
        )

    def meet_one(slot, rows, part, other, columns):
        scores = scored(slot, rows, other, columns)
        cost = penalty(slot, other)
        col_best[other, :, columns] = jnp.maximum(col_best[other, :, columns], fold_rows(scores) + cost)
        part[...] = jnp.maximum(part[...], fold_columns(scores) + cost)

    def meet(slot, start, size, low, high, halves=(), unroll=False):
        rows, every = pl.ds(start, size), pl.ds(0, rows_all)
        part = row_part.at[0:size, :]
        part[...] = jnp.full((size, 128), LOW, jnp.float32)
        for other in halves:
            meet_one(slot, rows, part, other, pl.ds(0, HALF))
        if unroll:
            for other in range(low, high):
                meet_one(slot, rows, part, other, every)
        else:

            def one(other, carry):
                meet_one(slot, rows, part, other, every)
                return carry

            lax.fori_loop(low, high, one, 0)
        best = jnp.max(part[...].T, axis=0, keepdims=True)
        row_best[slot, :, rows] = jnp.broadcast_to(best, (8, size))

    def own_normalise(index, carry):
        slot, start = PER + lax.div(index, 2), pl.multiple_of(lax.rem(index, 2) * HALF, HALF)
        normalise(slot, start, HALF, lambda rows: window[slot, rows, :])
        return carry

    lax.fori_loop(0, PER * 2, own_normalise, 0)

    def own_step(slot, carry):
        meet(slot, 0, rows_all, PER, slot)
        scores = scored(slot, pl.ds(0, rows_all), slot, pl.ds(0, rows_all))
        row_ids = lax.broadcasted_iota(jnp.int32, scores.shape, 0)
        col_ids = lax.broadcasted_iota(jnp.int32, scores.shape, 1)
        allowed = (row_ids < count_of(slot)) & (row_ids != col_ids)
        scores = jnp.where(allowed, scores, jnp.float32(LOW))
        col_best[slot] = jnp.maximum(col_best[slot], fold_rows(scores) + penalty(slot, slot))
        return carry

    lax.fori_loop(PER, 2 * PER, own_step, 0)

    for piece, (first, size) in enumerate(PIECES):
        for side, lent in ((0, l_left), (1, r_right)):
            swap(side, piece).wait()

            def choose(index, carry, side=side, lent=lent, first=first):
                rows = pl.ds(pl.multiple_of(first + index * 64, 64), 64)
                stage[side, rows, :] = jnp.where(lent, swapped[side, rows, :], stage[side, rows, :])
                return carry

            lax.fori_loop(0, size // 64, choose, 0)
            push(THIRD, side, piece).start()

    def take(step, side, pieces, low, high, halves=(), unroll=False):
        slot = 2 * PER + step if side == 0 else PER - 1 - step
        for piece in pieces:
            if step == FOURTH:
                pass_on(side, piece).wait_recv()
            elif step != THIRD:
                push(step, side, piece).wait_recv()
            normalise(slot, *PIECES[piece], lambda rows: raw[side, step, rows, :])
        start, size = PIECES[pieces[0]][0], sum(PIECES[piece][1] for piece in pieces)
        meet(slot, start, size, low, high, halves, unroll)

    both = (0, 1)
    own, right, left_next, right_next = PER, 2 * PER, PER - 1 - NEXT, 2 * PER + NEXT
    take(NEAR, 0, both, own, right)
    take(NEAR, 1, both, own + 1, right + 1)
    for piece in both:
        for side in (1, 0):
            push(THIRD, side, piece).wait_recv()
            pass_on(side, piece).start()
            push(NEXT, side, piece).start()
    take(THIRD, 0, both, own - 1, right)
    take(THIRD, 1, both, own + 2, right + 1)
    take(NEXT, 0, (0,), own - 1, right - 1)
    take(NEXT, 1, (0,), own + 2, right + 1, (right_next,))
    take(FOURTH, 0, both, own, own + 2)
    take(FOURTH, 1, both, own + 2, right)
    take(NEXT, 0, (1,), own - 1, right - 1, (left_next,), True)
    take(NEXT, 1, (1,), own + 2, right + 2, (), True)

    def best_of(slot):
        return jnp.maximum(row_best[slot, 0:1, :], jnp.max(col_best[slot], axis=0, keepdims=True))

    for block in range(PER):
        sent_best[0, block : block + 1, :] = best_of(block)
        sent_best[1, block : block + 1, :] = best_of(2 * PER + block)
    bests = [
        remote(sent_best.at[0], got_best.at[0], best_send.at[0], best_recv.at[0], LEFT),
        remote(sent_best.at[1], got_best.at[1], best_send.at[1], best_recv.at[1], RIGHT),
    ]
    for copy in bests:
        copy.start()

    for step in (NEAR, NEXT, THIRD):
        for piece in range(len(PIECES)):
            for side in range(2):
                push(step, side, piece).wait_send()
    for side in range(2):
        for piece in range(len(PIECES)):
            pass_on(side, piece).wait_send()

    for copy in bests:
        copy.wait()
    ids = lax.broadcasted_iota(jnp.int32, (1, rows_all), 1)
    for block in range(PER):
        best = jnp.maximum(best_of(PER + block), jnp.float32(-1.0))
        best = jnp.maximum(best, got_best[0, block : block + 1, :])
        best = jnp.maximum(best, got_best[1, block : block + 1, :])
        out[block : block + 1, :] = jnp.where(ids < counts[block], best, jnp.float32(0.0))


def solution(mesh):
    def per_device(embeddings, partners, cluster, counts):
        blocks, rows, width = embeddings.shape
        dma = pltpu.SemaphoreType.DMA
        return pl.pallas_call(
            kernel,
            out_shape=jax.ShapeDtypeStruct((blocks, rows), jnp.float32),
            in_specs=[pl.BlockSpec(memory_space=pl.ANY)] * 4,
            out_specs=pl.BlockSpec(memory_space=pltpu.VMEM),
            scratch_shapes=[
                pltpu.VMEM((SLOTS, rows, width), jnp.bfloat16),
                pltpu.VMEM((2, PER, rows, width), jnp.bfloat16),
                pltpu.VMEM((2, rows, width), jnp.bfloat16),
                pltpu.VMEM((2, rows, width), jnp.bfloat16),
                pltpu.VMEM(partners.shape, jnp.int32),
                pltpu.SMEM(cluster.shape, jnp.int32),
                pltpu.SMEM(counts.shape, jnp.int32),
                pltpu.VMEM((7, 16, 128), jnp.int32),
                pltpu.SMEM((7, 16, 128), jnp.int32),
                pltpu.VMEM((SLOTS, 8, rows), jnp.float32),
                pltpu.VMEM((rows, 128), jnp.float32),
                pltpu.VMEM((SLOTS, 8, rows), jnp.float32),
                pltpu.VMEM((2, PER, rows), jnp.float32),
                pltpu.VMEM((2, PER, rows), jnp.float32),
                dma((PER,)),
                dma((3,)),
                dma((2,)),
                dma((2, 3, 2)),
                dma((2, 3, 2)),
                dma((2, 2)),
                dma((2, 2)),
                dma((2, 2)),
                dma((2, 2)),
                dma((7,)),
                dma((7,)),
                dma,
                dma((2,)),
                dma((2,)),
            ],
            compiler_params=pltpu.CompilerParams(
                collective_id=0, has_side_effects=True, vmem_limit_bytes=60 * 2**20
            ),
        )(embeddings, partners, cluster, counts)

    return jax.shard_map(
        per_device,
        mesh=mesh,
        in_specs=(P(AXES, None, None), P(AXES, None), P(AXES), P(AXES)),
        out_specs=P(AXES, None),
        check_vma=False,
    )
```

time: 79.2 us -> 72.5 us (0.915)
  the two profiles are of different devices: /device:TPU:0 before, /device:TPU:225 now
where the time goes in v2:
time: 72.5 us; the launch traced here: 72.3 us
  Pallas kernels  71 us (98%)
  local copies, waits for them, and re-layouts  1.3 us (2%)
    pallas_call x1, Pallas kernels, per_device(): pl.pallas_call(kernel, out_shape=jax.ShapeDtypeStruct((blocks, rows), jnp...  71 us

profile of v2, /device:TPU:225, one launch (start us, length us, event | category | flops | bytes accessed | tf_op | source)
XLA Modules:
  0.0 72.3 jit_solution(15244987463358492440)
XLA Ops:
  0.0 71.0 %shard_map.46 = f32[4,512]{1,0:T(4,128)} custom-call(bf16[4,512,768]{2,1,0:T(8,128)(2,1)} %emb.1, s32[4,8]{1,0:T(4,128)} %partners_hbm.1, s32[4]{0:T(128)} %cluster_hbm.1, s32[4]{0:T(128)} %counts_hbm.1), custom_call_target="tpu_custom_call" | custom-call | tf_op jit(solution)/shard_map/pallas_call | solution.py:359
  71.0 1.3 %copy.6 = f32[4,512]{1,0:T(4,128)} copy(f32[4,512]{1,0:T(4,128)} %shard_map.46) | data formatting | bytes 16384

commit v3 on v2

--- a/solution.py
+++ b/solution.py
@@ -14,6 +14,7 @@
 LEFT, OWN, RIGHT, MATE_R, MATE_L, BEHIND, AHEAD = range(7)
 NEAR, NEXT, THIRD, FOURTH = range(4)
 PIECES = ((0, HALF), (HALF, HALF))
+LAP = 64
 
 
 def fold_rows(scores):
@@ -42,6 +43,7 @@
     cluster,
     counts,
     info,
+    own_facts,
     facts,
     col_best,
     row_part,
@@ -59,7 +61,9 @@
     pass_recv,
     info_send,
     info_recv,
+    own_facts_sem,
     facts_sem,
+    late_sem,
     best_send,
     best_recv,
 ):
@@ -86,11 +90,23 @@
         BEHIND: place(mate_l - 1),
         AHEAD: place(mate_r + 1),
     }
+    opens_lap = lax.rem(me, LAP) == 0
+    late_for = {
+        RIGHT: lax.rem(me, LAP) == LAP - 1,
+        MATE_L: lax.rem(me, LAP) == LAP - groups,
+        AHEAD: lax.rem(me, LAP) == LAP - 1 - groups,
+    }
     seen_as = {LEFT: RIGHT, RIGHT: LEFT, MATE_R: MATE_R, MATE_L: MATE_L, BEHIND: AHEAD, AHEAD: BEHIND}
 
     barrier = pltpu.get_barrier_semaphore()
     for role in where_is:
-        pl.semaphore_signal(barrier, inc=1, device_id=where_is[role], device_id_type=MESH)
+        if role in late_for:
+
+            @pl.when(jnp.logical_not(late_for[role]))
+            def _(role=role):
+                pl.semaphore_signal(barrier, inc=1, device_id=where_is[role], device_id_type=MESH)
+        else:
+            pl.semaphore_signal(barrier, inc=1, device_id=where_is[role], device_id_type=MESH)
 
     small = [
         pltpu.make_async_copy(partners_hbm, partners, small_sem.at[0]),
@@ -111,7 +127,14 @@
     for block in range(PER):
         info[OWN, PER + block : PER + block + 1, :] = jnp.full((1, 128), cluster[block], jnp.int32)
         info[OWN, 2 * PER + block : 2 * PER + block + 1, :] = jnp.full((1, 128), counts[block], jnp.int32)
-    pl.semaphore_wait(barrier, len(where_is))
+    to_own_facts = pltpu.make_async_copy(info.at[OWN], own_facts, own_facts_sem)
+    to_own_facts.start()
+    pl.semaphore_wait(barrier, jnp.where(opens_lap, len(where_is) - len(late_for), len(where_is)))
+    for role in late_for:
+
+        @pl.when(late_for[role])
+        def _(role=role):
+            pl.semaphore_signal(late_sem, inc=1, device_id=where_is[role], device_id_type=MESH)
 
     def remote(source, target, send_sem, recv_sem, role):
         return pltpu.make_async_remote_copy(
@@ -146,11 +169,6 @@
             MATE_R if side == 0 else MATE_L,
         )
 
-    infos = [
-        remote(info.at[OWN], info.at[seen_as[role]], info_send.at[role], info_recv.at[seen_as[role]], role)
-        for role in where_is
-    ]
-
     def swap(side, piece):
         rows = pl.ds(*PIECES[piece])
         return remote(
@@ -161,25 +179,33 @@
             MATE_L if side == 0 else MATE_R,
         )
 
-    for copy in infos:
-        copy.start()
+    infos = {
+        role: remote(info.at[OWN], info.at[seen_as[role]], info_send.at[role], info_recv.at[seen_as[role]], role)
+        for role in where_is
+    }
+    for role in (RIGHT, MATE_R, AHEAD):
+        infos[role].start()
     for piece in range(len(PIECES)):
-        for side in range(2):
-            swap(side, piece).start()
-
+        swap(1, piece).start()
+    push(NEAR, 1, 0).start()
+
+    @pl.when(opens_lap)
+    def _():
+        pl.semaphore_wait(late_sem, len(late_for))
+
+    for role in (LEFT, MATE_L, BEHIND):
+        infos[role].start()
     for piece in range(len(PIECES)):
-        for side in range(2):
-            push(NEAR, side, piece).start()
+        swap(0, piece).start()
+    push(NEAR, 0, 0).start()
+    push(NEAR, 1, 1).start()
+    push(NEAR, 0, 1).start()
 
     col_best[...] = jnp.full(col_best.shape, LOW, jnp.float32)
     row_best[...] = jnp.full(row_best.shape, LOW, jnp.float32)
-    for copy in infos:
-        copy.wait()
-    to_facts = pltpu.make_async_copy(info, facts, facts_sem)
-    to_facts.start()
     for copy in loads + stages:
         copy.wait()
-    to_facts.wait()
+    to_own_facts.wait()
 
     def cluster_of(device, block):
         return facts[device, PER + block, 0]
@@ -192,6 +218,97 @@
         keeps_left = spans_three & (is_first | jnp.logical_not(spans_all))
         return mate_spans_all & jnp.logical_not(keeps_left), mate_spans_all & keeps_left
 
+    def slot_cost(slot):
+        holds = jnp.where(slot == 2 * PER + THIRD, jnp.logical_not(r_left), True)
+        holds = jnp.where(slot == 2 * PER + FOURTH, mr_left, holds)
+        holds = jnp.where(slot == PER - 1 - THIRD, jnp.logical_not(l_right), holds)
+        return jnp.where(slot == PER - 1 - FOURTH, ml_right, holds)
+
+    def count_of(slot):
+        return facts[lax.div(slot, PER), 2 * PER + lax.rem(slot, PER), 0]
+
+    def penalty(slot, other):
+        first, second = jnp.minimum(slot, other), jnp.maximum(slot, other)
+        device_a, block_a = lax.div(first, PER), lax.rem(first, PER)
+        device_b, block_b = lax.div(second, PER), lax.rem(second, PER)
+        listed = facts[device_a, block_a, second - first] >= 0
+        same = cluster_of(device_a, block_a) == cluster_of(device_b, block_b)
+        held = slot_cost(slot) & slot_cost(other)
+        return jnp.where(listed & same & held, jnp.float32(0.0), jnp.float32(LOW))
+
+    def own_count(slot):
+        return own_facts[2 * PER + slot - PER, 0]
+
+    def own_penalty(slot, other):
+        listed = own_facts[other - PER, slot - other] >= 0
+        same = own_facts[slot, 0] == own_facts[other, 0]
+        return jnp.where(listed & same, jnp.float32(0.0), jnp.float32(LOW))
+
+    def normalise(slot, start, size, load, count):
+        rows = pl.ds(start, size)
+        floats = load(rows).astype(jnp.float32)
+        unit = floats * lax.rsqrt(jnp.sum(floats * floats, axis=-1, keepdims=True) + 1e-06)
+        head = window[slot, 0:16, :].astype(jnp.float32)[0:1, :]
+        head = jnp.where(start == 0, unit[0:1, :], head)
+        ids = start + lax.broadcasted_iota(jnp.int32, (size, 1), 0)
+        window[slot, rows, :] = jnp.where(ids < count, unit, head).astype(jnp.bfloat16)
+
+    def scored(slot, rows, other, columns):
+        return lax.dot_general(
+            window[slot, rows, :],
+            window[other, columns, :],
+            (((1,), (1,)), ((), ())),
+            preferred_element_type=jnp.float32,
+        )
+
+    def meet_one(slot, rows, part, other, columns, cost):
+        scores = scored(slot, rows, other, columns)
+        col_best[other, :, columns] = jnp.maximum(col_best[other, :, columns], fold_rows(scores) + cost)
+        part[...] = jnp.maximum(part[...], fold_columns(scores) + cost)
+
+    def meet(slot, start, size, low, high, halves=(), unroll=False, cost=penalty):
+        rows, every = pl.ds(start, size), pl.ds(0, rows_all)
+        part = row_part.at[0:size, :]
+        part[...] = jnp.full((size, 128), LOW, jnp.float32)
+        for other in halves:
+            meet_one(slot, rows, part, other, pl.ds(0, HALF), cost(slot, other))
+        if unroll:
+            for other in range(low, high):
+                meet_one(slot, rows, part, other, every, cost(slot, other))
+        else:
+
+            def one(other, carry):
+                meet_one(slot, rows, part, other, every, cost(slot, other))
+                return carry
+
+            lax.fori_loop(low, high, one, 0)
+        best = jnp.max(part[...].T, axis=0, keepdims=True)
+        row_best[slot, :, rows] = jnp.broadcast_to(best, (8, size))
+
+    def own_normalise(index, carry):
+        slot, start = PER + lax.div(index, 2), pl.multiple_of(lax.rem(index, 2) * HALF, HALF)
+        normalise(slot, start, HALF, lambda rows: window[slot, rows, :], own_count(slot))
+        return carry
+
+    lax.fori_loop(0, PER * 2, own_normalise, 0)
+
+    def own_step(slot, carry):
+        meet(slot, 0, rows_all, PER, slot, cost=own_penalty)
+        scores = scored(slot, pl.ds(0, rows_all), slot, pl.ds(0, rows_all))
+        row_ids = lax.broadcasted_iota(jnp.int32, scores.shape, 0)
+        col_ids = lax.broadcasted_iota(jnp.int32, scores.shape, 1)
+        allowed = (row_ids < own_count(slot)) & (row_ids != col_ids)
+        scores = jnp.where(allowed, scores, jnp.float32(LOW))
+        col_best[slot] = jnp.maximum(col_best[slot], fold_rows(scores) + own_penalty(slot, slot))
+        return carry
+
+    lax.fori_loop(PER, 2 * PER, own_step, 0)
+
+    for role in infos:
+        infos[role].wait()
+    to_facts = pltpu.make_async_copy(info, facts, facts_sem)
+    to_facts.start()
+    to_facts.wait()
     whole_r, three_r = spans(OWN, RIGHT)
     whole_mr, three_mr = spans(MATE_R, AHEAD)
     whole_l, three_l = spans(LEFT, OWN)
@@ -201,85 +318,6 @@
     l_left, l_right = third_is_lent(first_l, whole_l, three_l, whole_ml)
     _, ml_right = third_is_lent(jnp.logical_not(first_l), whole_ml, three_ml, whole_l)
 
-    def slot_cost(slot):
-        holds = jnp.where(slot == 2 * PER + THIRD, jnp.logical_not(r_left), True)
-        holds = jnp.where(slot == 2 * PER + FOURTH, mr_left, holds)
-        holds = jnp.where(slot == PER - 1 - THIRD, jnp.logical_not(l_right), holds)
-        return jnp.where(slot == PER - 1 - FOURTH, ml_right, holds)
-
-    def count_of(slot):
-        return facts[lax.div(slot, PER), 2 * PER + lax.rem(slot, PER), 0]
-
-    def penalty(slot, other):
-        first, second = jnp.minimum(slot, other), jnp.maximum(slot, other)
-        device_a, block_a = lax.div(first, PER), lax.rem(first, PER)
-        device_b, block_b = lax.div(second, PER), lax.rem(second, PER)
-        listed = facts[device_a, block_a, second - first] >= 0
-        same = cluster_of(device_a, block_a) == cluster_of(device_b, block_b)
-        held = slot_cost(slot) & slot_cost(other)
-        return jnp.where(listed & same & held, jnp.float32(0.0), jnp.float32(LOW))
-
-    def normalise(slot, start, size, load):
-        rows = pl.ds(start, size)
-        floats = load(rows).astype(jnp.float32)
-        unit = floats * lax.rsqrt(jnp.sum(floats * floats, axis=-1, keepdims=True) + 1e-06)
-        head = window[slot, 0:16, :].astype(jnp.float32)[0:1, :]
-        head = jnp.where(start == 0, unit[0:1, :], head)
-        ids = start + lax.broadcasted_iota(jnp.int32, (size, 1), 0)
-        window[slot, rows, :] = jnp.where(ids < count_of(slot), unit, head).astype(jnp.bfloat16)
-
-    def scored(slot, rows, other, columns):
-        return lax.dot_general(
-            window[slot, rows, :],
-            window[other, columns, :],
-            (((1,), (1,)), ((), ())),
-            preferred_element_type=jnp.float32,
-        )
-
-    def meet_one(slot, rows, part, other, columns):
-        scores = scored(slot, rows, other, columns)
-        cost = penalty(slot, other)
-        col_best[other, :, columns] = jnp.maximum(col_best[other, :, columns], fold_rows(scores) + cost)
-        part[...] = jnp.maximum(part[...], fold_columns(scores) + cost)
-
-    def meet(slot, start, size, low, high, halves=(), unroll=False):
-        rows, every = pl.ds(start, size), pl.ds(0, rows_all)
-        part = row_part.at[0:size, :]
-        part[...] = jnp.full((size, 128), LOW, jnp.float32)
-        for other in halves:
-            meet_one(slot, rows, part, other, pl.ds(0, HALF))
-        if unroll:
-            for other in range(low, high):
-                meet_one(slot, rows, part, other, every)
-        else:
-
-            def one(other, carry):
-                meet_one(slot, rows, part, other, every)
-                return carry
-
-            lax.fori_loop(low, high, one, 0)
-        best = jnp.max(part[...].T, axis=0, keepdims=True)
-        row_best[slot, :, rows] = jnp.broadcast_to(best, (8, size))
-
-    def own_normalise(index, carry):
-        slot, start = PER + lax.div(index, 2), pl.multiple_of(lax.rem(index, 2) * HALF, HALF)
-        normalise(slot, start, HALF, lambda rows: window[slot, rows, :])
-        return carry
-
-    lax.fori_loop(0, PER * 2, own_normalise, 0)
-
-    def own_step(slot, carry):
-        meet(slot, 0, rows_all, PER, slot)
-        scores = scored(slot, pl.ds(0, rows_all), slot, pl.ds(0, rows_all))
-        row_ids = lax.broadcasted_iota(jnp.int32, scores.shape, 0)
-        col_ids = lax.broadcasted_iota(jnp.int32, scores.shape, 1)
-        allowed = (row_ids < count_of(slot)) & (row_ids != col_ids)
-        scores = jnp.where(allowed, scores, jnp.float32(LOW))
-        col_best[slot] = jnp.maximum(col_best[slot], fold_rows(scores) + penalty(slot, slot))
-        return carry
-
-    lax.fori_loop(PER, 2 * PER, own_step, 0)
-
     for piece, (first, size) in enumerate(PIECES):
         for side, lent in ((0, l_left), (1, r_right)):
             swap(side, piece).wait()
@@ -299,7 +337,7 @@
                 pass_on(side, piece).wait_recv()
             elif step != THIRD:
                 push(step, side, piece).wait_recv()
-            normalise(slot, *PIECES[piece], lambda rows: raw[side, step, rows, :])
+            normalise(slot, *PIECES[piece], lambda rows: raw[side, step, rows, :], count_of(slot))
         start, size = PIECES[pieces[0]][0], sum(PIECES[piece][1] for piece in pieces)
         meet(slot, start, size, low, high, halves, unroll)
 
@@ -312,12 +350,14 @@
             push(THIRD, side, piece).wait_recv()
             pass_on(side, piece).start()
             push(NEXT, side, piece).start()
-    take(THIRD, 0, both, own - 1, right)
-    take(THIRD, 1, both, own + 2, right + 1)
-    take(NEXT, 0, (0,), own - 1, right - 1)
-    take(NEXT, 1, (0,), own + 2, right + 1, (right_next,))
-    take(FOURTH, 0, both, own, own + 2)
-    take(FOURTH, 1, both, own + 2, right)
+        take(THIRD, 0, (piece,), own - 1, right, (), True)
+        take(THIRD, 1, (piece,), own + 2, right + 1, (), True)
+    take(FOURTH, 0, (0,), own, own + 2, (), True)
+    take(FOURTH, 1, (0,), own + 2, right, (), True)
+    take(NEXT, 0, (0,), own - 1, right - 1, (), True)
+    take(NEXT, 1, (0,), own + 2, right + 1, (right_next,), True)
+    take(FOURTH, 0, (1,), own, own + 2, (), True)
+    take(FOURTH, 1, (1,), own + 2, right, (), True)
     take(NEXT, 0, (1,), own - 1, right - 1, (left_next,), True)
     take(NEXT, 1, (1,), own + 2, right + 2, (), True)
 
@@ -370,6 +410,7 @@
                 pltpu.SMEM(cluster.shape, jnp.int32),
                 pltpu.SMEM(counts.shape, jnp.int32),
                 pltpu.VMEM((7, 16, 128), jnp.int32),
+                pltpu.SMEM((16, 128), jnp.int32),
                 pltpu.SMEM((7, 16, 128), jnp.int32),
                 pltpu.VMEM((SLOTS, 8, rows), jnp.float32),
                 pltpu.VMEM((rows, 128), jnp.float32),
@@ -388,6 +429,8 @@
                 dma((7,)),
                 dma((7,)),
                 dma,
+                dma,
+                pltpu.SemaphoreType.REGULAR,
                 dma((2,)),
                 dma((2,)),
             ],

time: 72.5 us -> 69.5 us (0.959)
  the two profiles are of different devices: /device:TPU:225 before, /device:TPU:2 now
where the time goes in v3:
time: 69.5 us; the launch traced here: 69.3 us
  Pallas kernels  68 us (98%)
  local copies, waits for them, and re-layouts  1.3 us (2%)
    pallas_call x1, Pallas kernels, per_device(): pl.pallas_call(kernel, out_shape=jax.ShapeDtypeStruct((blocks, rows), jnp...  68 us

profile of v3, /device:TPU:2, one launch (start us, length us, event | category | flops | bytes accessed | tf_op | source)
XLA Modules:
  0.0 69.3 jit_solution(4225861695282032812)
XLA Ops:
  0.0 68.0 %shard_map.46 = f32[4,512]{1,0:T(4,128)} custom-call(bf16[4,512,768]{2,1,0:T(8,128)(2,1)} %emb.1, s32[4,8]{1,0:T(4,128)} %partners_hbm.1, s32[4]{0:T(128)} %cluster_hbm.1, s32[4]{0:T(128)} %counts_hbm.1), custom_call_target="tpu_custom_call" | custom-call | tf_op jit(solution)/shard_map/pallas_call | solution.py:399
  68.0 1.3 %copy.6 = f32[4,512]{1,0:T(4,128)} copy(f32[4,512]{1,0:T(4,128)} %shard_map.46) | data formatting | bytes 16384

commit v4 on v3

--- a/solution.py
+++ b/solution.py
@@ -14,6 +14,7 @@
 LEFT, OWN, RIGHT, MATE_R, MATE_L, BEHIND, AHEAD = range(7)
 NEAR, NEXT, THIRD, FOURTH = range(4)
 PIECES = ((0, HALF), (HALF, HALF))
+PARTS = ((0, HALF // 2), (HALF // 2, HALF // 2), (HALF, HALF))
 LAP = 64
 
 
@@ -147,7 +148,7 @@
         )
 
     def push(step, side, piece):
-        start, size = PIECES[piece]
+        start, size = PARTS[piece] if step == NEXT else PIECES[piece]
         rows = pl.ds(start, size)
         block = step if side == 0 else PER - 1 - step
         source = stage.at[side, rows, :] if step == THIRD else emb.at[block, rows, :]
@@ -318,6 +319,17 @@
     l_left, l_right = third_is_lent(first_l, whole_l, three_l, whole_ml)
     _, ml_right = third_is_lent(jnp.logical_not(first_l), whole_ml, three_ml, whole_l)
 
+    same_lap = (lax.rem(me, LAP) != 0, lax.rem(me, LAP) != LAP - 1)
+    goes_first = ((lax.rem(me, pool) == 0) & same_lap[0], (lax.rem(me, pool) == pool - 1) & same_lap[1])
+    turns = ((lax.rem(me, groups) == 0) & same_lap[0], (lax.rem(me, groups) == groups - 1) & same_lap[1])
+    both, every_part = (0, 1), (0, 1, 2)
+
+    def push_if(condition, step, side, pieces):
+        @pl.when(condition)
+        def _():
+            for piece in pieces:
+                push(step, side, piece).start()
+
     for piece, (first, size) in enumerate(PIECES):
         for side, lent in ((0, l_left), (1, r_right)):
             swap(side, piece).wait()
@@ -328,28 +340,37 @@
                 return carry
 
             lax.fori_loop(0, size // 64, choose, 0)
-            push(THIRD, side, piece).start()
+            push_if(jnp.logical_not(goes_first[side]), THIRD, side, (piece,))
+    for side in (0, 1):
+        push_if(jnp.logical_not(goes_first[side]), NEXT, side, every_part)
 
     def take(step, side, pieces, low, high, halves=(), unroll=False):
         slot = 2 * PER + step if side == 0 else PER - 1 - step
         for piece in pieces:
             if step == FOURTH:
                 pass_on(side, piece).wait_recv()
-            elif step != THIRD:
-                push(step, side, piece).wait_recv()
+            elif step == NEXT:
+                for part in ((0, 1), (2,))[piece]:
+                    push(NEXT, side, part).wait_recv()
             normalise(slot, *PIECES[piece], lambda rows: raw[side, step, rows, :], count_of(slot))
         start, size = PIECES[pieces[0]][0], sum(PIECES[piece][1] for piece in pieces)
         meet(slot, start, size, low, high, halves, unroll)
 
-    both = (0, 1)
     own, right, left_next, right_next = PER, 2 * PER, PER - 1 - NEXT, 2 * PER + NEXT
+    for piece in both:
+        for side in both:
+            push(NEAR, side, piece).wait_recv()
+    for side in both:
+        push_if(goes_first[side], THIRD, side, both)
     take(NEAR, 0, both, own, right)
     take(NEAR, 1, both, own + 1, right + 1)
     for piece in both:
         for side in (1, 0):
             push(THIRD, side, piece).wait_recv()
             pass_on(side, piece).start()
-            push(NEXT, side, piece).start()
+        if piece == 1:
+            for side in both:
+                push_if(goes_first[side], NEXT, side, every_part)
         take(THIRD, 0, (piece,), own - 1, right, (), True)
         take(THIRD, 1, (piece,), own + 2, right + 1, (), True)
     take(FOURTH, 0, (0,), own, own + 2, (), True)
@@ -375,7 +396,7 @@
         copy.start()
 
     for step in (NEAR, NEXT, THIRD):
-        for piece in range(len(PIECES)):
+        for piece in range(len(PARTS if step == NEXT else PIECES)):
             for side in range(2):
                 push(step, side, piece).wait_send()
     for side in range(2):
@@ -420,8 +441,8 @@
                 dma((PER,)),
                 dma((3,)),
                 dma((2,)),
-                dma((2, 3, 2)),
-                dma((2, 3, 2)),
+                dma((2, 3, 3)),
+                dma((2, 3, 3)),
                 dma((2, 2)),
                 dma((2, 2)),
                 dma((2, 2)),

time: 69.5 us -> 67.6 us (0.973)
  the two profiles are of different devices: /device:TPU:2 before, /device:TPU:0 now
where the time goes in v4:
time: 67.6 us; the launch traced here: 67.5 us
  Pallas kernels  66.2 us (98%)
  local copies, waits for them, and re-layouts  1.3 us (2%)
    pallas_call x1, Pallas kernels, per_device(): pl.pallas_call(kernel, out_shape=jax.ShapeDtypeStruct((blocks, rows), jnp...  66.2 us

profile of v4, /device:TPU:0, one launch (start us, length us, event | category | flops | bytes accessed | tf_op | source)
XLA Modules:
  0.0 67.5 jit_solution(2766125492288390432)
XLA Ops:
  0.0 66.2 %shard_map.46 = f32[4,512]{1,0:T(4,128)} custom-call(bf16[4,512,768]{2,1,0:T(8,128)(2,1)} %emb.1, s32[4,8]{1,0:T(4,128)} %partners_hbm.1, s32[4]{0:T(128)} %cluster_hbm.1, s32[4]{0:T(128)} %counts_hbm.1), custom_call_target="tpu_custom_call" | custom-call | tf_op jit(solution)/shard_map/pallas_call | solution.py:420
  66.2 1.3 %copy.6 = f32[4,512]{1,0:T(4,128)} copy(f32[4,512]{1,0:T(4,128)} %shard_map.46) | data formatting | bytes 16384

commit v5 on v4

--- a/solution.py
+++ b/solution.py
@@ -184,8 +184,13 @@
         role: remote(info.at[OWN], info.at[seen_as[role]], info_send.at[role], info_recv.at[seen_as[role]], role)
         for role in where_is
     }
+    def greet_left():
+        for role in (LEFT, MATE_L, BEHIND):
+            infos[role].start()
+
     for role in (RIGHT, MATE_R, AHEAD):
         infos[role].start()
+    pl.when(jnp.logical_not(opens_lap))(greet_left)
     for piece in range(len(PIECES)):
         swap(1, piece).start()
     push(NEAR, 1, 0).start()
@@ -193,9 +198,8 @@
     @pl.when(opens_lap)
     def _():
         pl.semaphore_wait(late_sem, len(late_for))
-
-    for role in (LEFT, MATE_L, BEHIND):
-        infos[role].start()
+        greet_left()
+
     for piece in range(len(PIECES)):
         swap(0, piece).start()
     push(NEAR, 0, 0).start()
@@ -365,7 +369,7 @@
     take(NEAR, 0, both, own, right)
     take(NEAR, 1, both, own + 1, right + 1)
     for piece in both:
-        for side in (1, 0):
+        for side in (0, 1):
             push(THIRD, side, piece).wait_recv()
             pass_on(side, piece).start()
         if piece == 1:

time: 67.6 us -> 67.6 us (level)
  no operation moved by 1% of the time
where the time goes in v5:
time: 67.6 us; the launch traced here: 67.5 us
  Pallas kernels  66.2 us (98%)
  local copies, waits for them, and re-layouts  1.3 us (2%)
    pallas_call x1, Pallas kernels, per_device(): pl.pallas_call(kernel, out_shape=jax.ShapeDtypeStruct((blocks, rows), jnp...  66.2 us

profile of v5, /device:TPU:0, one launch (start us, length us, event | category | flops | bytes accessed | tf_op | source)
XLA Modules:
  0.0 67.5 jit_solution(10984596179781490339)
XLA Ops:
  0.0 66.2 %shard_map.46 = f32[4,512]{1,0:T(4,128)} custom-call(bf16[4,512,768]{2,1,0:T(8,128)(2,1)} %emb.1, s32[4,8]{1,0:T(4,128)} %partners_hbm.1, s32[4]{0:T(128)} %cluster_hbm.1, s32[4]{0:T(128)} %counts_hbm.1), custom_call_target="tpu_custom_call" | custom-call | tf_op jit(solution)/shard_map/pallas_call | solution.py:424
  66.2 1.3 %copy.6 = f32[4,512]{1,0:T(4,128)} copy(f32[4,512]{1,0:T(4,128)} %shard_map.46) | data formatting | bytes 16384

commit v6 on v5

--- a/solution.py
+++ b/solution.py
@@ -362,11 +362,12 @@
 
     own, right, left_next, right_next = PER, 2 * PER, PER - 1 - NEXT, 2 * PER + NEXT
     for piece in both:
-        for side in both:
-            push(NEAR, side, piece).wait_recv()
-    for side in both:
-        push_if(goes_first[side], THIRD, side, both)
+        push(NEAR, 0, piece).wait_recv()
+    push_if(goes_first[0], THIRD, 0, both)
     take(NEAR, 0, both, own, right)
+    for piece in both:
+        push(NEAR, 1, piece).wait_recv()
+    push_if(goes_first[1], THIRD, 1, both)
     take(NEAR, 1, both, own + 1, right + 1)
     for piece in both:
         for side in (0, 1):
@@ -383,14 +384,19 @@
     take(NEXT, 1, (0,), own + 2, right + 1, (right_next,), True)
     take(FOURTH, 0, (1,), own, own + 2, (), True)
     take(FOURTH, 1, (1,), own + 2, right, (), True)
+    def best_of(slot):
+        return jnp.maximum(row_best[slot, 0:1, :], jnp.max(col_best[slot], axis=0, keepdims=True))
+
+    for block in (0, 1):
+        sent_best[0, block : block + 1, :] = best_of(block)
+    for block in (2, 3):
+        sent_best[1, block : block + 1, :] = best_of(2 * PER + block)
     take(NEXT, 0, (1,), own - 1, right - 1, (left_next,), True)
     take(NEXT, 1, (1,), own + 2, right + 2, (), True)
 
-    def best_of(slot):
-        return jnp.maximum(row_best[slot, 0:1, :], jnp.max(col_best[slot], axis=0, keepdims=True))
-
-    for block in range(PER):
+    for block in (2, 3):
         sent_best[0, block : block + 1, :] = best_of(block)
+    for block in (0, 1):
         sent_best[1, block : block + 1, :] = best_of(2 * PER + block)
     bests = [
         remote(sent_best.at[0], got_best.at[0], best_send.at[0], best_recv.at[0], LEFT),

time: 67.6 us -> 67.6 us (level)
  no operation moved by 1% of the time
where the time goes in v6:
time: 67.6 us; the launch traced here: 67.5 us
  Pallas kernels  66.2 us (98%)
  local copies, waits for them, and re-layouts  1.3 us (2%)
    pallas_call x1, Pallas kernels, per_device(): pl.pallas_call(kernel, out_shape=jax.ShapeDtypeStruct((blocks, rows), jnp...  66.2 us

profile of v6, /device:TPU:0, one launch (start us, length us, event | category | flops | bytes accessed | tf_op | source)
XLA Modules:
  0.0 67.5 jit_solution(14869522777775429404)
XLA Ops:
  0.0 66.2 %shard_map.46 = f32[4,512]{1,0:T(4,128)} custom-call(bf16[4,512,768]{2,1,0:T(8,128)(2,1)} %emb.1, s32[4,8]{1,0:T(4,128)} %partners_hbm.1, s32[4]{0:T(128)} %cluster_hbm.1, s32[4]{0:T(128)} %counts_hbm.1), custom_call_target="tpu_custom_call" | custom-call | tf_op jit(solution)/shard_map/pallas_call | solution.py:430
  66.2 1.3 %copy.6 = f32[4,512]{1,0:T(4,128)} copy(f32[4,512]{1,0:T(4,128)} %shard_map.46) | data formatting | bytes 16384
